TPU v7x, 256 devices: a whole 4x4x8 slice. The times are simulated.
256 devices in a mesh: gx: 32 (over z, y), gy: 8 (over x, core).
Axes of the slice: x: 4, y: 4, z: 8, core: 2. Of those that a mesh axis runs over, the one named last changes fastest.
Arguments:
- positions: float32 [3, 1048576], P(None, ('gx', 'gy')), may hold values from 0 to 512, as said below
- mass: float32 [1048576], P(('gx', 'gy')), may hold values from 0.5 to 2
- smoothing: float32 [1048576], P(('gx', 'gy')), may hold values from 1.5 to 3
- energy: float32 [1048576], P(('gx', 'gy')), may hold values from 0.5 to 4
- destination: int32 [1048576, 1], P(('gx', 'gy')), may hold values from 0 to 255, as said below
- pairs: int32 [2, 221184], P(None, ('gx', 'gy')), may hold values from 0 to 63, as said below
- pair_count: int32 [256], P(('gx', 'gy')), may hold values from 432 to 864, as said below
Outputs:
- density: float32 [1048576], P(('gx', 'gy'))
- accel: float32 [3, 1048576], P(None, ('gx', 'gy'))
Inputs may be any that keep to these rules, and one draw needn't show every extreme that they name: `destination`: the 4096 particles of every domain name each domain exactly 16 times. `positions`: each particle lies in the box of its new domain (i, j): first coordinate in [16 i, 16 (i + 1)], second in [16 j, 16 (j + 1)], third in [0, 16]. `pairs`: row 0 holds target tiles below 32, row 1 source tiles below 32 + 4 * 8 (tiles from 32 on are ghost tiles); domain d's list is columns d * 864 to (d + 1) * 864 - 1, and slots from pair_count[d] on are unused. `pair_count`: some domain uses all 864 slots.
All inputs are finite; a program needn't handle non-finite values.
Results may differ from a plain program's by a relative error of at most 0.0005.
Values sent between devices are 32-bit elements; how exact they have to be, the bound alone decides.
No kernel may reach another device: no remote copies, remote signals or barrier semaphores. Data moves between devices by JAX's collectives and lax.ppermute only.
A program may use at most 64 MiB of HBM per device.

v0:
```python
import math

import jax
import jax.numpy as jnp
from jax import lax
from jax.sharding import PartitionSpec as P

GT = 8


KERNEL_NORM = 21.0 / (2.0 * math.pi)
GAMMA_LESS = 2.0 / 3.0


def extended(block, sides, width):
    for axis, dim in sides:
        count = lax.axis_size(axis)
        forward = [(i, i + 1) for i in range(count - 1)]
        backward = [(target, source) for source, target in forward]
        low = lax.ppermute(
            lax.slice_in_dim(block, block.shape[dim] - width, None, axis=dim), axis, forward
        )
        high = lax.ppermute(lax.slice_in_dim(block, 0, width, axis=dim), axis, backward)
        block = jnp.concatenate([low, block, high], axis=dim)
    return block


def neighbour_rows(ghosts):
    return jnp.concatenate(
        [ghosts[..., 0, 1, :], ghosts[..., 2, 1, :], ghosts[..., 1, 0, :], ghosts[..., 1, 2, :]],
        axis=-1,
    )


def density_domain(pool, pair_list, count, own_tiles):
    slots = pair_list.shape[1]
    group_size = slots // own_tiles
    tile_rows = pool.shape[2]

    def density_advance(block, totals):
        start = block * group_size
        target = lax.dynamic_slice_in_dim(pair_list[0], start, group_size)
        source = lax.dynamic_slice_in_dim(pair_list[1], start, group_size)
        active = start + jnp.arange(group_size, dtype=jnp.int32) < count
        nearer = pool[target]
        farther = pool[source]
        dist_sq = jnp.zeros((group_size, tile_rows, tile_rows), jnp.float32)
        for component in range(3):
            offset = nearer[:, component, :, None] - farther[:, component, None, :]
            dist_sq = dist_sq + offset * offset
        radius = nearer[:, 4, :, None]
        ratio = jnp.sqrt(dist_sq) / radius
        falloff = jnp.maximum(1.0 - ratio, 0.0)
        kernel = KERNEL_NORM / (radius * radius * radius) * falloff**4 * (1.0 + 4.0 * ratio)
        summed = jnp.sum(kernel * farther[:, 3, None, :], axis=2)
        summed = jnp.where(active[:, None], summed, 0.0)
        return totals.at[target].add(summed)

    group_total = (count + group_size - 1) // group_size
    totals = lax.fori_loop(
        0, group_total, density_advance, jnp.zeros((own_tiles, tile_rows), jnp.float32)
    )
    own = pool[:own_tiles]
    radius = own[:, 4, :]
    self_term = own[:, 3, :] * KERNEL_NORM / (radius * radius * radius)
    return (totals + self_term).reshape(-1)


def accel_domain(pool, press_pool, pair_list, count, own_tiles):
    slots = pair_list.shape[1]
    group_size = slots // own_tiles
    tile_rows = pool.shape[2]

    def accel_advance(block, totals):
        start = block * group_size
        target = lax.dynamic_slice_in_dim(pair_list[0], start, group_size)
        source = lax.dynamic_slice_in_dim(pair_list[1], start, group_size)
        active = start + jnp.arange(group_size, dtype=jnp.int32) < count
        nearer = pool[target]
        farther = pool[source]
        press_own = press_pool[target]
        press_far = press_pool[source]
        dist_sq = jnp.zeros((group_size, tile_rows, tile_rows), jnp.float32)
        for component in range(3):
            offset = nearer[:, component, :, None] - farther[:, component, None, :]
            dist_sq = dist_sq + offset * offset
        mean_radius = 0.5 * (nearer[:, 4, :, None] + farther[:, 4, None, :])
        ratio = jnp.sqrt(dist_sq) / mean_radius
        falloff = jnp.maximum(1.0 - ratio, 0.0)
        slope = -20.0 * KERNEL_NORM * falloff**3 / mean_radius**5
        coupling = farther[:, 3, None, :] * (press_own[:, :, None] + press_far[:, None, :]) * slope
        summed = jnp.sum(coupling, axis=2)
        parts_list = []
        for component in range(3):
            pulled = jnp.sum(coupling * farther[:, component, None, :], axis=2)
            parts_list.append(-(nearer[:, component, :] * summed - pulled))
        result = jnp.stack(parts_list, axis=1)
        result = jnp.where(active[:, None, None], result, 0.0)
        return totals.at[target].add(result)

    group_total = (count + group_size - 1) // group_size
    totals = lax.fori_loop(
        0, group_total, accel_advance, jnp.zeros((own_tiles, 3, tile_rows), jnp.float32)
    )
    return jnp.transpose(totals, (1, 0, 2)).reshape(3, -1)


def local(positions, mass, smoothing, energy, destination, pairs, pair_count):
    across = lax.axis_size("gx")
    beside = lax.axis_size("gy")
    domains = across * beside
    dev_rows = mass.shape[0]
    slot_count = dev_rows // domains
    tile_rows = 128
    own_tiles = dev_rows // tile_rows
    edge_rows = GT * tile_rows
    fields = jnp.concatenate([positions, mass[None], smoothing[None], energy[None]], 0)
    ranking = jnp.argsort(destination[:, 0], stable=True)
    outgoing = jnp.transpose(fields[:, ranking].reshape(6, domains, slot_count), (1, 0, 2))
    outgoing = outgoing.reshape(across, beside, 6 * slot_count)
    moved = lax.all_to_all(
        lax.all_to_all(outgoing, "gx", split_axis=0, concat_axis=0, tiled=True),
        "gy",
        split_axis=1,
        concat_axis=1,
        tiled=True,
    )
    settled = jnp.transpose(moved.reshape(domains, 6, slot_count), (1, 0, 2)).reshape(6, dev_rows)
    boundary = settled[:, :edge_rows].reshape(6, 1, 1, edge_rows)
    ghosts = extended(boundary, (("gx", 1), ("gy", 2)), 1)
    extra = neighbour_rows(ghosts)
    pool = jnp.concatenate([settled, extra], 1).reshape(6, own_tiles + 4 * GT, tile_rows)
    pool = jnp.transpose(pool, (1, 0, 2))
    count = pair_count[0]
    density = density_domain(pool, pairs, count, own_tiles)
    press = GAMMA_LESS * settled[5] / density
    press_edge = press[:edge_rows].reshape(1, 1, edge_rows)
    press_ghosts = extended(press_edge, (("gx", 0), ("gy", 1)), 1)
    press_extra = neighbour_rows(press_ghosts)
    press_pool = jnp.concatenate([press, press_extra], 0).reshape(own_tiles + 4 * GT, tile_rows)
    accel = accel_domain(pool, press_pool, pairs, count, own_tiles)
    return (density, accel)


def solution(mesh):
    placed = (
        P(None, ("gx", "gy")),
        P(("gx", "gy")),
        P(("gx", "gy")),
        P(("gx", "gy")),
        P(("gx", "gy"), None),
        P(None, ("gx", "gy")),
        P(("gx", "gy")),
    )
    return jax.shard_map(
        local,
        mesh=mesh,
        in_specs=placed,
        out_specs=(P(("gx", "gy")), P(None, ("gx", "gy"))),
        check_vma=False,
    )
```

profile of v0, /device:TPU:121, one launch (start us, length us, event | category | flops | bytes accessed | tf_op | source)
XLA Modules:
  0.0 629.5 jit_solution(3920355547435640939)
XLA Ops:
  2.3 5.8 sort.17
  8.0 14.1 %gather_fusion.6 = f32[4096,6]{1,0:T(8,128)} fusion(f32[6,4096]{0,1:T(8,128)S(1)} %copy.37, s32[4096]{0:T(1024)S(1)} %fusion.21), kind=kCustom, calls=%fused_computation.6 | custom fusion | bytes 212992 | tf_op jit(solution)/shard_map/gather | solution.py:119
  25.6 15.0 %all_to_all.10 = f32[32,8,96]{2,1,0:T(8,128)S(1)} all-to-all(f32[32,8,96]{2,1,0:T(8,128)S(1)} %reshape.243), channel_id=1, replica_groups=mesh['gx'=32,'gy'=8] {'gx'}, dimensions={0} | all-to-all | bytes 196608 | tf_op jit(solution)/shard_map/all_to_all | solution.py:122
  41.2 6.3 %all-to-all-start.1 = ((f32[32,8,96]{2,0,1:T(8,128)}), f32[32,8,96]{2,0,1:T(8,128)S(1)}, u32[]{:S(2)}, u32[]{:S(2)}) async-start(f32[32,8,96]{2,0,1:T(8,128)} %copy.39), calls=%async_computation.1 | async-start | bytes 262144 | tf_op jit(solution)/shard_map/all_to_all | solution.py:121
  60.0 5.5 collective-permute-done.1
  75.8 196.8 %while.20 = (s32[]{:T(128)}, f32[32,128]{1,0:T(8,128)S(1)}, s32[]{:T(128)}, s32[2,864]{1,0:T(2,128)S(1)}, s32[]{:T(128)}, /*index=5*/f32[64,6,128]{2,1,0:T(8,128...) while((s32[]{:T(128)}, f32[32,128]{1,0:T(8,128)S(1)}, s32[]{:T(128)}, ...), condition=%wide.region_4.5_spmd, body=%wide.region_1.4_spmd.sunk | while | flops 8421140 | bytes 996498 | solution.py:60
  290.9 338.0 %while.21 = (s32[]{:T(128)}, f32[32,3,128]{2,1,0:T(4,128)S(1)}, s32[]{:T(128)}, s32[2,864]{1,0:T(2,128)S(1)}, s32[]{:T(128)}, /*index=5*/f32[64,6,128]{2,1,0:T(8...) while((s32[]{:T(128)}, f32[32,3,128]{2,1,0:T(4,128)S(1)}, ...), condition=%wide.region_11.12_spmd, body=%wide.region_5.11_spmd.sunk | while | flops 13332116 | bytes 1461229 | solution.py:102
  293.6 5.3 multiply_reduce_fusion.7
  304.1 5.3 multiply_reduce_fusion.7
  314.7 5.3 multiply_reduce_fusion.7
  325.2 5.3 multiply_reduce_fusion.7
  346.4 5.3 multiply_reduce_fusion.7
  356.9 5.3 multiply_reduce_fusion.7
  367.5 5.3 multiply_reduce_fusion.7
  378.0 5.3 multiply_reduce_fusion.7
  388.6 5.3 multiply_reduce_fusion.7
  399.2 5.3 multiply_reduce_fusion.7
  409.7 5.3 multiply_reduce_fusion.7
  420.3 5.3 multiply_reduce_fusion.7
  441.4 5.3 multiply_reduce_fusion.7
  452.0 5.3 multiply_reduce_fusion.7
  462.5 5.3 multiply_reduce_fusion.7
  473.1 5.3 multiply_reduce_fusion.7
  483.7 5.3 multiply_reduce_fusion.7
  (1445 shorter events, 479.6 us)
Async XLA Ops:
  0.6 1.6 copy-start.2
  41.2 11.6 %all-to-all-start.1 = ((f32[32,8,96]{2,0,1:T(8,128)}), f32[32,8,96]{2,0,1:T(8,128)S(1)}, u32[]{:S(2)}, u32[]{:S(2)}) async-start(f32[32,8,96]{2,0,1:T(8,128)} %copy.39), calls=%async_computation.1 | async-start | bytes 262144 | tf_op jit(solution)/shard_map/all_to_all | solution.py:121
  53.2 22.6 %copy-start.1 = (s32[2,864]{1,0:T(2,128)S(1)}, s32[2,864]{1,0:T(2,128)}, u32[]{:S(2)}) copy-start(s32[2,864]{1,0:T(2,128)} %param.16) | copy-start | bytes 20740
  53.8 6.2 collective-permute-start
  57.5 8.0 %collective-permute-start.1 = (f32[6,1,1,1024]{3,0,2,1:T(8,128)S(1)}, f32[6,1,1,1024]{3,0,2,1:T(8,128)S(1)}, u32[]{:S(2)}, u32[]{:S(2)}) collective-permute-start(f32[6,1,1,1024]{3,0,2,1:T(8,128)S(1)} %slice_bitcast_fusion.2), channel_id=1, source_target_pairs={{8,0},{16,8},{24,16},{32,24},{40,32},{48,40},{56,48},{64,56},{72,6... | collective-permute-start | bytes 73736 | tf_op jit(solution)/shard_map/ppermute | solution.py:23
  65.4 6.3 %collective-permute-start.2 = (f32[6,3,1,1024]{3,0,2,1:T(8,128)S(1)}, f32[6,3,1,1024]{3,0,2,1:T(8,128)S(1)}, u32[]{:S(2)}, u32[]{:S(2)}) collective-permute-start(f32[6,3,1,1024]{3,0,2,1:T(8,128)S(1)} %pad_maximum_fusion.1), channel_id=1, source_target_pairs={{0,1},{1,2},{2,3},{3,4},{4,5},{5,6},{6,7},{8,9},{9,10},{10,11},{11... | collective-permute-start | bytes 221192 | tf_op jit(solution)/shard_map/ppermute | solution.py:20
  69.8 5.9 collective-permute-start.3
  273.3 5.3 collective-permute-start.4
  275.2 7.7 %collective-permute-start.5 = (f32[1,1,1024]{2,1,0:T(1,128)S(1)}, f32[1,1,1024]{2,1,0:T(1,128)S(1)}, u32[]{:S(2)}, u32[]{:S(2)}) collective-permute-start(f32[1,1,1024]{2,1,0:T(1,128)S(1)} %bitcast.197), channel_id=1, source_target_pairs={{8,0},{16,8},{24,16},{32,24},{40,32},{48,40},{56,48},{64,56},{72,6... | collective-permute-start | bytes 12296 | tf_op jit(solution)/shard_map/ppermute | solution.py:23
  282.9 4.9 collective-permute-start.6
  285.9 5.0 collective-permute-start.7
  628.9 0.6 copy-start
where the time goes:
time: 631 us; the launch traced here: 630 us
  other arithmetic  413 us (65%)
  local copies, waits for them, and re-layouts  139 us (22%)
  starting transfers between devices  28.4 us (5%)
  waiting for transfers between devices  21.3 us (3%)
  blocking collectives  15 us (2%)
  loops' own time  11 us (2%)
    reduce_sum x32, other arithmetic, accel_advance(): pulled = jnp.sum(coupling * farther[:, component, None, :], axis=2)  171 us
    reduce_sum x32, other arithmetic, density_advance(): summed = jnp.sum(kernel * farther[:, 3, None, :], axis=2)  101 us
    scatter-add x32, other arithmetic, accel_advance(): return totals.at[target].add(result)  54.7 us
    scatter-add x32, other arithmetic, density_advance(): return totals.at[target].add(summed)  25.1 us
    lt x32, other arithmetic, density_advance(): active = start + jnp.arange(group_size, dtype=jnp.int32) < count  20.9 us
    lt x32, other arithmetic, accel_advance(): active = start + jnp.arange(group_size, dtype=jnp.int32) < count  20.9 us
    gather x32, local copies, waits for them, and re-layouts, accel_advance(): nearer = pool[target]  18.5 us
    gather x32, local copies, waits for them, and re-layouts, density_advance(): nearer = pool[target]  18.5 us
  transfers between devices with their start and end apart: 9, of which 5 were waited for; matrix products, arithmetic and copies ran while one was open for 0% of the time, Pallas kernels for 0%

commit v1 on v0

v1 whole, which is shorter than its diff:
```python
import functools
import math

import jax
import jax.numpy as jnp
from jax import lax
from jax.experimental import pallas as pl
from jax.experimental.pallas import tpu as pltpu
from jax.sharding import PartitionSpec as P

F32, BF16, I32 = jnp.float32, jnp.bfloat16, jnp.int32
TILE = 128
OWN = 32
GT = 8
ALL = OWN + 4 * GT
CAP = 16
BOX = 16.0
HALF = 8.0
KEYS = 48
GROUP = 2
KERNEL_NORM = 21.0 / (2.0 * math.pi)
GAMMA_LESS = 2.0 / 3.0
STARTS = (0, 1024, 1280, 2048)

NT = (((1,), (1,)), ((), ()))
NN = (((1,), (0,)), ((), ()))


def iota(shape, axis):
    return lax.broadcasted_iota(I32, shape, axis)


def dot(a, b, dims=NN):
    return lax.dot_general(a, b, dims, preferred_element_type=F32)


def pieces(v):
    one = v.astype(BF16).astype(F32)
    rest = v - one
    two = rest.astype(BF16).astype(F32)
    return one, two, rest - two


def dispatch_kernel(pos, mass, smooth, energy, dest, out):
    width = 256
    n = pos.shape[1]
    row = iota((width, width), 0)
    upper = (row < iota((width, width), 1)).astype(F32).astype(BF16)
    ones = jnp.ones((width, width), BF16)
    carry = jnp.zeros((width, width), F32)
    total = jnp.zeros((width, 128), F32)
    ranks = iota((CAP, width), 0)
    for b in range(n // width):
        at = slice(b * width, (b + 1) * width)
        mine = row == dest[:, at]
        hot = jnp.where(mine, 1.0, 0.0)
        hot16 = hot.astype(BF16)
        before = dot(hot16, upper) + carry
        carry = carry + dot(hot16, ones)
        rank = jnp.sum(hot * before, axis=0, keepdims=True).astype(I32)
        sel = ranks == rank
        rows = [pos[0:1, at], pos[1:2, at], pos[2:3, at], mass[:, at], smooth[:, at], energy[:, at]]
        spread = jnp.concatenate(
            [jnp.where(sel, v, 0.0) for v in rows] + [jnp.zeros((2 * CAP, width), F32)], axis=0
        )
        for piece in pieces(spread):
            total = total + dot(hot16, piece.astype(BF16), NT)
    out[...] = total


def list_kernel(count, pairs, out):
    slots = pairs.shape[1]
    target, source = pairs[0:1, :], pairs[1:2, :]
    ghost = (source >= OWN).astype(I32)
    line = jnp.where(iota((1, slots), 1) < count[0], target + OWN * ghost, -1)
    column = source - OWN * ghost
    lines = jnp.where(iota((ALL, slots), 0) == line, 1.0, 0.0).astype(BF16)
    columns = jnp.where(iota((OWN, slots), 0) == column, 1.0, 0.0).astype(BF16)
    times = dot(columns, lines, NT)
    has = jnp.where(times > 0.0, 1.0, 0.0)
    has16 = has.astype(BF16)
    lower = jnp.where(iota((OWN, OWN), 0) > iota((OWN, OWN), 1), 1.0, 0.0).astype(BF16)
    within = dot(lower, has16)
    per_line = dot(jnp.ones((OWN, OWN), BF16), has16)
    la, lb = iota((ALL, ALL), 0), iota((ALL, ALL), 1)

    def section(k):
        return (k >= OWN).astype(I32) + (k >= OWN + GT).astype(I32)

    ahead = jnp.where((la < lb) & (section(la) == section(lb)), 1.0, 0.0).astype(BF16)
    lane = iota((OWN, ALL), 1)
    start = jnp.where(lane < OWN, STARTS[0], jnp.where(lane < OWN + GT, STARTS[1], STARTS[2]))
    place = within + dot(per_line.astype(BF16), ahead) + start.astype(F32)
    high = jnp.floor(place * (1.0 / 128.0))
    low = (place - 128.0 * high).astype(I32)
    high = jnp.where(has > 0.0, high.astype(I32), -1)
    sub = iota((OWN, ALL), 0)
    code = times * 2048.0 + ((lane % OWN) * 64 + sub + jnp.where(lane >= OWN, OWN, 0)).astype(F32)
    total = jnp.zeros((48, 128), F32)
    parts = pieces(code)
    for k in range(OWN):
        picked = iota((16, ALL), 0) == high[k : k + 1]
        left = jnp.concatenate([jnp.where(picked, p[k : k + 1], 0.0) for p in parts], axis=0)
        right = jnp.where(iota((128, ALL), 0) == low[k : k + 1], 1.0, 0.0)
        total = total + dot(left.astype(BF16), right.astype(BF16), NT)
    out[0:16] = (total[0:16] + total[16:32] + total[32:48]).astype(I32)
    lane1 = iota((1, ALL), 1)
    tallies = []
    for k in range(3):
        tallies.append(jnp.sum(jnp.where(section(lane1) == k, per_line[0:1], 0.0), axis=1, keepdims=True))
    r = iota((8, 128), 0)
    counts = jnp.where(r == 0, tallies[0], jnp.where(r == 1, tallies[1], tallies[2]))
    out[16:24] = counts.astype(I32)


def fields_of(block, shift):
    sub, lane = iota((8, 128), 0), iota((8, 128), 1) // CAP
    for bit in (1, 2, 4):
        up = pltpu.roll(pltpu.roll(block, bit, 0), 128 - CAP * bit, 1)
        down = up if bit == 4 else pltpu.roll(pltpu.roll(block, 8 - bit, 0), CAP * bit, 1)
        i, j = (sub // bit) % 2, (lane // bit) % 2
        block = jnp.where(i == j, block, jnp.where(i == 1, up, down))
    block = block - shift
    square = jnp.sum(jnp.where(sub < 3, block * block, 0.0), axis=0, keepdims=True)
    return jnp.where(sub == 6, square, jnp.where(sub == 7, 1.0, block))


def source_factor(v):
    a, b, c = pieces(v)
    return jnp.concatenate([a, a, a, b, b, c], axis=0)


def target_factor(u):
    a, b, c = pieces(u)
    return jnp.concatenate([a, b, c, a, b, a], axis=0)


def coefficients(v):
    sub = iota((8, 128), 0)
    return jnp.where(sub < 3, -2.0 * v, jnp.where(sub == 6, 1.0, jnp.where(sub == 7, v[6:7], 0.0)))


def entry(codes, e):
    code = codes[e >> 7, e & 127]
    return (code >> 6) & (OWN - 1), code & (ALL - 1), code >> 11


def sweep(codes, section, product, process, buffers):
    start = STARTS[section]
    last = STARTS[section + 1] - 1
    count = codes[16 + section, 0]

    def load(group, buffer):
        for k in range(GROUP):
            t, s, _ = entry(codes, jnp.minimum(start + group * GROUP + k, last))
            buffer[k] = product(t, s)

    def work(group, buffer):
        for k in range(GROUP):
            e = start + group * GROUP + k
            t, s, times = entry(codes, jnp.minimum(e, last))
            process(t, s, jnp.where(e < start + count, times, 0), buffer, k)

    load(0, buffers[0])

    def body(i, unused):
        load(2 * i + 1, buffers[1])
        work(2 * i, buffers[0])
        load(2 * i + 2, buffers[0])
        work(2 * i + 1, buffers[1])
        return unused

    lax.fori_loop(0, (count + 2 * GROUP - 1) // (2 * GROUP), body, 0)


def density_kernel(codes, centre, moved, g0, g1, g2, g3, density, press, fields, factors, right, sums, buf0, buf1):
    sub = iota((8, 128), 0)
    shift = jnp.where(sub == 0, centre[0], jnp.where(sub == 1, centre[1], jnp.where(sub == 2, HALF, 0.0)))

    def place(tile, block):
        v = fields_of(block, shift)
        fields[tile] = v
        factors[tile] = jnp.transpose(source_factor(v)).astype(BF16)
        return v

    weigh = jnp.where(sub == 3, 4.0, 0.0)
    none = jnp.zeros((8, 128), F32)
    weigh = jnp.concatenate([weigh, none, none, weigh, none, weigh], axis=0).astype(BF16)

    def own(tile, unused):
        v = place(tile, moved[pl.ds(pl.multiple_of(tile * 8, 8), 8)])
        h = v[4:5]
        right[tile, :, 0:128] = target_factor(coefficients(v) * (1.0 / (h * h))).astype(BF16)
        right[tile, :, 128:256] = weigh
        sums[tile] = none
        return unused

    lax.fori_loop(0, OWN, own, 0)
    for k, ghost in enumerate((g0, g1, g2, g3)):

        def other(tile, unused):
            place(OWN + k * GT + tile, ghost[pl.ds(pl.multiple_of(tile * 8, 8), 8)])
            return unused

        lax.fori_loop(0, GT, other, 0)

    def product(t, s):
        return dot(factors[s], right[t])

    def process(t, s, times, buffer, k):
        ratio_sq = jnp.maximum(buffer[k, :, 0:128], 1e-30)
        ratio = ratio_sq * lax.rsqrt(ratio_sq)
        falloff = jnp.maximum(1.0 - ratio, 0.0)
        falloff = falloff * falloff
        falloff = falloff * falloff
        term = falloff * (ratio + 0.25) * buffer[k, :, 128:256]
        sums[t] += jnp.sum(term.reshape(16, 8, 128), axis=0) * jnp.full((8, 128), times, I32).astype(F32)

    for section in range(3):
        sweep(codes, section, product, process, (buf0, buf1))
    total = jnp.sum(sums[...], axis=1)
    h = fields[0:OWN, 4, :]
    result = KERNEL_NORM / (h * h * h) * (total + fields[0:OWN, 3, :])
    density[...] = result
    press[...] = GAMMA_LESS * fields[0:OWN, 5, :] / result


def accel_kernel(codes, fields, factors, press, p0, p1, p2, p3, accel, right, pulls, sums, buf0, buf1):
    sub = iota((8, 128), 0)
    none = jnp.zeros((8, 128), F32)

    def pull(tile, p):
        v = fields[tile]
        x = jnp.where(sub < 4, pltpu.roll(v, 1, 0), pltpu.roll(v, 5, 0))
        x = jnp.where(sub % 4 == 0, 1.0, x) * v[3:4]
        x = jnp.where(sub < 4, x, x * p)
        both = jnp.concatenate([*pieces(x), none], axis=0).astype(BF16)
        pulls[tile, :, 0:128] = both
        pulls[tile, :, 128:256] = both
        return v

    def own(tile, unused):
        v = pull(tile, press[pl.ds(tile, 1)])
        right[tile, :, 0:128] = target_factor(coefficients(v)).astype(BF16)
        h = jnp.where(sub == 4, 1.0, jnp.where(sub == 7, v[4:5], 0.0))
        right[tile, :, 128:256] = target_factor(h).astype(BF16)
        sums[tile] = jnp.zeros((32, 128), F32)
        return unused

    lax.fori_loop(0, OWN, own, 0)
    for k, ghost in enumerate((p0, p1, p2, p3)):

        def other(tile, unused):
            pull(OWN + k * GT + tile, ghost[pl.ds(tile, 1)])
            return unused

        lax.fori_loop(0, GT, other, 0)

    def product(t, s):
        return dot(factors[s], right[t])

    def process(t, s, times, buffer, k):
        dist_sq = jnp.maximum(buffer[k, :, 0:128], 1e-30)
        near = 1.0 / buffer[k, :, 128:256]
        near_sq = near * near
        gap = jnp.maximum(near - dist_sq * lax.rsqrt(dist_sq) * (2.0 * near_sq), 0.0)
        slope = gap * gap * gap * near_sq
        first = slope.astype(BF16)
        second = (slope - first.astype(F32)).astype(BF16)
        both = jnp.concatenate([first, second], axis=0)
        sums[t] += dot(pulls[s], both) * jnp.full((32, 128), times, I32).astype(F32)

    for section in range(3):
        sweep(codes, section, product, process, (buf0, buf1))

    def finish(tile, unused):
        v = fields[tile]
        s = sums[tile]
        s = s[0:8] + s[8:16] + s[16:24]
        p = press[pl.ds(tile, 1)]
        a = p * (v * s[0:1] - pltpu.roll(s, 7, 0)) + (v * s[4:5] - pltpu.roll(s, 3, 0))
        accel[:, pl.ds(pl.multiple_of(tile * 128, 128), 128)] = a[0:3] * (640.0 * KERNEL_NORM)
        return unused

    lax.fori_loop(0, OWN, finish, 0)


def call(kernel, shapes, scratch=(), smem=0, args=(), limit=40):
    specs = [pl.BlockSpec(memory_space=pltpu.SMEM)] * smem
    specs += [pl.BlockSpec(memory_space=pltpu.VMEM)] * (len(args) - smem)
    return pl.pallas_call(
        kernel,
        out_shape=[jax.ShapeDtypeStruct(s, d) for s, d in shapes],
        in_specs=specs,
        out_specs=[pl.BlockSpec(memory_space=pltpu.VMEM)] * len(shapes),
        scratch_shapes=list(scratch),
        compiler_params=pltpu.CompilerParams(vmem_limit_bytes=limit * 2**20),
    )(*args)


def around(edge):
    taken = []
    for axis in ("gx", "gy"):
        count = lax.axis_size(axis)
        forward = [(i, i + 1) for i in range(count - 1)]
        taken.append(lax.ppermute(edge, axis, forward))
        taken.append(lax.ppermute(edge, axis, [(b, a) for a, b in forward]))
    return taken


def local(positions, mass, smoothing, energy, destination, pairs, pair_count):
    rows = mass.shape[0]
    flat = [a.reshape(1, rows) for a in (mass, smoothing, energy, destination)]
    (outgoing,) = call(dispatch_kernel, [((256, 128), F32)], args=(positions, *flat))
    (codes,) = call(list_kernel, [((24, 128), I32)], smem=1, args=(pair_count, pairs))
    moved = lax.all_to_all(outgoing, ("gx", "gy"), split_axis=0, concat_axis=0, tiled=True)
    ghosts = around(moved[: GT * 8])
    centre = jnp.stack([lax.axis_index("gx"), lax.axis_index("gy")]).astype(F32) * BOX + HALF
    density, press, fields, factors = call(
        density_kernel,
        [((OWN, 128), F32), ((OWN, 128), F32), ((ALL, 8, 128), F32), ((ALL, 128, KEYS), BF16)],
        scratch=[
            pltpu.VMEM((OWN, KEYS, 256), BF16),
            pltpu.VMEM((OWN, 8, 128), F32),
            pltpu.VMEM((GROUP, 128, 256), F32),
            pltpu.VMEM((GROUP, 128, 256), F32),
        ],
        smem=2,
        args=(codes, centre, moved, *ghosts),
    )
    presses = around(press[:GT])
    (accel,) = call(
        accel_kernel,
        [((3, rows), F32)],
        scratch=[
            pltpu.VMEM((OWN, KEYS, 256), BF16),
            pltpu.VMEM((ALL, 32, 256), BF16),
            pltpu.VMEM((OWN, 32, 128), F32),
            pltpu.VMEM((GROUP, 128, 256), F32),
            pltpu.VMEM((GROUP, 128, 256), F32),
        ],
        smem=1,
        args=(codes, fields, factors, press, *presses),
    )
    return density.reshape(rows), accel


def solution(mesh):
    placed = (
        P(None, ("gx", "gy")),
        P(("gx", "gy")),
        P(("gx", "gy")),
        P(("gx", "gy")),
        P(("gx", "gy"), None),
        P(None, ("gx", "gy")),
        P(("gx", "gy")),
    )
    return jax.shard_map(
        local,
        mesh=mesh,
        in_specs=placed,
        out_specs=(P(("gx", "gy")), P(None, ("gx", "gy"))),
        check_vma=False,
    )
```

time: 631 us -> 195 us (0.31)
  the two profiles are of different devices: /device:TPU:121 before, /device:TPU:43 now
where the time goes in v1:
time: 195 us; the launch traced here: 193 us
  Pallas kernels  137 us (70%)
  starting transfers between devices  36.9 us (19%)
  waiting for transfers between devices  13.1 us (7%)
  local copies, waits for them, and re-layouts  4.39 us (2%)
    pallas_call x4, Pallas kernels, call(): pl.pallas_call(kernel, out_shape=[jax.ShapeDtypeStruct(s, d) for s, d in...  137 us
    all_to_all x1, starting transfers between devices, local(): lax.all_to_all(outgoing, ('gx', 'gy'), split_axis=0, concat_axis=0, tiled...  14.6 us
    ppermute x4, starting transfers between devices, around(): taken.append(lax.ppermute(edge, axis, forward))  11.3 us
    ppermute x4, starting transfers between devices, around(): taken.append(lax.ppermute(edge, axis, [(b, a) for a, b in forward]))  11 us
    all_to_all x1, waiting for transfers between devices, local(): lax.all_to_all(outgoing, ('gx', 'gy'), split_axis=0, concat_axis=0, tiled...  10.5 us
    unnamed x12, local copies, waits for them, and re-layouts  4.39 us
  transfers between devices with their start and end apart: 9, of which 3 were waited for; matrix products, arithmetic and copies ran while one was open for 0% of the time, Pallas kernels for 1%

profile of v1, /device:TPU:43, one launch (start us, length us, event | category | flops | bytes accessed | tf_op | source)
XLA Modules:
  0.0 192.9 jit_solution(5431260261838323785)
XLA Ops:
  0.6 0.8 copy-done
  1.5 0.7 copy-done.1
  2.2 0.7 copy-done.2
  2.9 0.7 copy-done.3
  3.6 0.7 copy-done.4
  4.3 5.1 %shard_map.87 = f32[256,128]{1,0:T(8,128)} custom-call(f32[3,4096]{1,0:T(4,128)S(1)} %copy-done, f32[1,4096]{1,0:T(1,128)S(1)} %bitcast.16, f32[1,4096]{1,0:T(1,128)S(1)} %bitcast.17, f32[1,4096]{1,0:T(1,128)S(1)} %bitcast.18, s32[1,4096]{1,0:T(1,128)S(1)} %bitcast.19), custom_call_target="tpu_custom_call" | custom-call | tf_op jit(solution)/shard_map/pallas_call | solution.py:291
  9.5 14.6 %all-to-all-start = ((f32[256,1,128]{2,1,0:T(1,128)}), f32[256,1,128]{2,1,0:T(1,128)S(1)}, u32[]{:S(2)}, u32[]{:S(2)}) async-start(f32[256,1,128]{2,1,0:T(1,128)} %bitcast.7), calls=%async_computation | async-start | bytes 262144 | tf_op jit(solution)/shard_map/all_to_all | solution.py:316
  24.1 10.5 %all-to-all-done = f32[256,1,128]{2,1,0:T(1,128)S(1)} async-done(((f32[256,1,128]{2,1,0:T(1,128)}), f32[256,1,128]{2,1,0:T(1,128)S(1)}, u32[]{:S(2)}, u32[]{:S(2)}) %all-to-all-start) | async-done | bytes 131104 | tf_op jit(solution)/shard_map/all_to_all | solution.py:316
  34.6 2.1 %collective-permute-start.3 = (f32[64,128]{1,0:T(8,128)S(1)}, f32[64,128]{1,0:T(8,128)S(1)}, u32[]{:S(2)}, u32[]{:S(2)}) collective-permute-start(f32[64,128]{1,0:T(8,128)S(1)} %slice_bitcast_fusion), channel_id=1, source_target_pairs={{1,0},{2,1},{3,2},{4,3},{5,4},{6,5},{7,6},{9,8},{10,9},{11,10},{12... | collective-permute-start | bytes 98312 | tf_op jit(solution)/shard_map/ppermute | solution.py:307
  36.8 3.4 %collective-permute-start.2 = (f32[64,128]{1,0:T(8,128)S(1)}, f32[64,128]{1,0:T(8,128)S(1)}, u32[]{:S(2)}, u32[]{:S(2)}) collective-permute-start(f32[64,128]{1,0:T(8,128)S(1)} %slice_bitcast_fusion), channel_id=1, source_target_pairs={{0,1},{1,2},{2,3},{3,4},{4,5},{5,6},{6,7},{8,9},{9,10},{10,11},{11... | collective-permute-start | bytes 98312 | tf_op jit(solution)/shard_map/ppermute | solution.py:306
  40.2 2.9 %collective-permute-start.1 = (f32[64,128]{1,0:T(8,128)S(1)}, f32[64,128]{1,0:T(8,128)S(1)}, u32[]{:S(2)}, u32[]{:S(2)}) collective-permute-start(f32[64,128]{1,0:T(8,128)S(1)} %slice_bitcast_fusion), channel_id=1, source_target_pairs={{8,0},{16,8},{24,16},{32,24},{40,32},{48,40},{56,48},{64,56},{72,6... | collective-permute-start | bytes 98312 | tf_op jit(solution)/shard_map/ppermute | solution.py:307
  43.1 2.4 %collective-permute-start = (f32[64,128]{1,0:T(8,128)S(1)}, f32[64,128]{1,0:T(8,128)S(1)}, u32[]{:S(2)}, u32[]{:S(2)}) collective-permute-start(f32[64,128]{1,0:T(8,128)S(1)} %slice_bitcast_fusion), channel_id=1, source_target_pairs={{0,8},{8,16},{16,24},{24,32},{32,40},{40,48},{48,56},{56,64},{64,7... | collective-permute-start | bytes 98312 | tf_op jit(solution)/shard_map/ppermute | solution.py:306
  45.5 0.1 fusion.1.centre
  46.2 0.0 copy-start.5
  46.2 0.7 copy-done.5
  46.9 1.2 shard_map.86.codes
  48.1 0.1 collective-permute-done.2.g2
  48.2 61.7 %shard_map.88 = (f32[32,128]{1,0:T(8,128)}, f32[32,128]{1,0:T(8,128)S(1)}, f32[64,8,128]{2,1,0:T(8,128)S(1)}, bf16[64,128,48]{2,1,0:T(8,128)(2,1)S(1)}) custom-call(s32[24,128]{1,0:T(8,128)S(1)} %shard_map.86.codes, f32[2]{0:T(128)S(1)} %fusion.1.centre, f32[256,128]{1,0:T(8,128)S(1)} %bitcast.15, f32[64,128]{1,0:T(8,128)S(1)} %collective-permute-done.g0, ...), custom_call_target="tpu_custom_call" | custom-call | tf_op jit(solution)/shard_map/pallas_call | solution.py:291
  109.8 1.9 collective-permute-start.7
  111.8 3.6 %collective-permute-start.6 = (f32[8,128]{1,0:T(8,128)S(1)}, f32[8,128]{1,0:T(8,128)S(1)}, u32[]{:S(2)}, u32[]{:S(2)}) collective-permute-start(f32[8,128]{1,0:T(8,128)S(1)} %slice.11), channel_id=1, source_target_pairs={{0,1},{1,2},{2,3},{3,4},{4,5},{5,6},{6,7},{8,9},{9,10},{10,11},{11... | collective-permute-start | bytes 12296 | tf_op jit(solution)/shard_map/ppermute | solution.py:306
  115.4 4.0 %collective-permute-start.5 = (f32[8,128]{1,0:T(8,128)S(1)}, f32[8,128]{1,0:T(8,128)S(1)}, u32[]{:S(2)}, u32[]{:S(2)}) collective-permute-start(f32[8,128]{1,0:T(8,128)S(1)} %slice.11), channel_id=1, source_target_pairs={{8,0},{16,8},{24,16},{32,24},{40,32},{48,40},{56,48},{64,56},{72,6... | collective-permute-start | bytes 12296 | tf_op jit(solution)/shard_map/ppermute | solution.py:307
  119.4 1.9 collective-permute-start.4
  121.4 2.6 %collective-permute-done.4.p0 = f32[8,128]{1,0:T(8,128)S(1)} collective-permute-done((f32[8,128]{1,0:T(8,128)S(1)}, f32[8,128]{1,0:T(8,128)S(1)}, u32[]{:S(2)}, u32[]{:S(2)}) %collective-permute-start.4) | collective-permute-done | bytes 4128 | tf_op jit(solution)/shard_map/ppermute | solution.py:306
  124.0 69.0 %shard_map.89 = f32[3,4096]{1,0:T(4,128)} custom-call(s32[24,128]{1,0:T(8,128)S(1)} %shard_map.86.codes, f32[64,8,128]{2,1,0:T(8,128)S(1)} %get-tuple-element.7.fields, bf16[64,128,48]{2,1,0:T(8,128)(2,1)S(1)} %get-tuple-element.8.factors, f32[32,128]{1,0:T(8,128)S(1)} %get-tuple-element.9.press, f32[8,128]{1,0:T(8,128)S(1)} %collective-permute-done.4.p0, ...), custom_call_target="tpu_custom_call" | custom-call | tf_op jit(solution)/shard_map/pallas_call | solution.py:291
  (13 shorter events, 0.0 us)
Async XLA Ops:
  0.6 0.8 copy-start
  1.5 0.7 copy-start.1
  2.2 0.7 copy-start.2
  2.9 0.7 copy-start.3
  3.6 0.7 copy-start.4
  9.5 25.1 %all-to-all-start = ((f32[256,1,128]{2,1,0:T(1,128)}), f32[256,1,128]{2,1,0:T(1,128)S(1)}, u32[]{:S(2)}, u32[]{:S(2)}) async-start(f32[256,1,128]{2,1,0:T(1,128)} %bitcast.7), calls=%async_computation | async-start | bytes 262144 | tf_op jit(solution)/shard_map/all_to_all | solution.py:316
  34.6 13.5 %collective-permute-start.3 = (f32[64,128]{1,0:T(8,128)S(1)}, f32[64,128]{1,0:T(8,128)S(1)}, u32[]{:S(2)}, u32[]{:S(2)}) collective-permute-start(f32[64,128]{1,0:T(8,128)S(1)} %slice_bitcast_fusion), channel_id=1, source_target_pairs={{1,0},{2,1},{3,2},{4,3},{5,4},{6,5},{7,6},{9,8},{10,9},{11,10},{12... | collective-permute-start | bytes 98312 | tf_op jit(solution)/shard_map/ppermute | solution.py:307
  36.8 11.4 %collective-permute-start.2 = (f32[64,128]{1,0:T(8,128)S(1)}, f32[64,128]{1,0:T(8,128)S(1)}, u32[]{:S(2)}, u32[]{:S(2)}) collective-permute-start(f32[64,128]{1,0:T(8,128)S(1)} %slice_bitcast_fusion), channel_id=1, source_target_pairs={{0,1},{1,2},{2,3},{3,4},{4,5},{5,6},{6,7},{8,9},{9,10},{10,11},{11... | collective-permute-start | bytes 98312 | tf_op jit(solution)/shard_map/ppermute | solution.py:306
  40.2 8.0 %collective-permute-start.1 = (f32[64,128]{1,0:T(8,128)S(1)}, f32[64,128]{1,0:T(8,128)S(1)}, u32[]{:S(2)}, u32[]{:S(2)}) collective-permute-start(f32[64,128]{1,0:T(8,128)S(1)} %slice_bitcast_fusion), channel_id=1, source_target_pairs={{8,0},{16,8},{24,16},{32,24},{40,32},{48,40},{56,48},{64,56},{72,6... | collective-permute-start | bytes 98312 | tf_op jit(solution)/shard_map/ppermute | solution.py:307
  43.1 5.1 %collective-permute-start = (f32[64,128]{1,0:T(8,128)S(1)}, f32[64,128]{1,0:T(8,128)S(1)}, u32[]{:S(2)}, u32[]{:S(2)}) collective-permute-start(f32[64,128]{1,0:T(8,128)S(1)} %slice_bitcast_fusion), channel_id=1, source_target_pairs={{0,8},{8,16},{16,24},{24,32},{32,40},{40,48},{48,56},{56,64},{64,7... | collective-permute-start | bytes 98312 | tf_op jit(solution)/shard_map/ppermute | solution.py:306
  46.2 0.7 copy-start.5
  109.8 11.5 %collective-permute-start.7 = (f32[8,128]{1,0:T(8,128)S(1)}, f32[8,128]{1,0:T(8,128)S(1)}, u32[]{:S(2)}, u32[]{:S(2)}) collective-permute-start(f32[8,128]{1,0:T(8,128)S(1)} %slice.11), channel_id=1, source_target_pairs={{1,0},{2,1},{3,2},{4,3},{5,4},{6,5},{7,6},{9,8},{10,9},{11,10},{12... | collective-permute-start | bytes 12296 | tf_op jit(solution)/shard_map/ppermute | solution.py:307
  111.8 9.6 %collective-permute-start.6 = (f32[8,128]{1,0:T(8,128)S(1)}, f32[8,128]{1,0:T(8,128)S(1)}, u32[]{:S(2)}, u32[]{:S(2)}) collective-permute-start(f32[8,128]{1,0:T(8,128)S(1)} %slice.11), channel_id=1, source_target_pairs={{0,1},{1,2},{2,3},{3,4},{4,5},{5,6},{6,7},{8,9},{9,10},{10,11},{11... | collective-permute-start | bytes 12296 | tf_op jit(solution)/shard_map/ppermute | solution.py:306
  115.4 6.0 %collective-permute-start.5 = (f32[8,128]{1,0:T(8,128)S(1)}, f32[8,128]{1,0:T(8,128)S(1)}, u32[]{:S(2)}, u32[]{:S(2)}) collective-permute-start(f32[8,128]{1,0:T(8,128)S(1)} %slice.11), channel_id=1, source_target_pairs={{8,0},{16,8},{24,16},{32,24},{40,32},{48,40},{56,48},{64,56},{72,6... | collective-permute-start | bytes 12296 | tf_op jit(solution)/shard_map/ppermute | solution.py:307
  119.4 4.5 %collective-permute-start.4 = (f32[8,128]{1,0:T(8,128)S(1)}, f32[8,128]{1,0:T(8,128)S(1)}, u32[]{:S(2)}, u32[]{:S(2)}) collective-permute-start(f32[8,128]{1,0:T(8,128)S(1)} %slice.11), channel_id=1, source_target_pairs={{0,8},{8,16},{16,24},{24,32},{32,40},{40,48},{48,56},{56,64},{64,7... | collective-permute-start | bytes 12296 | tf_op jit(solution)/shard_map/ppermute | solution.py:306

commit v2 on v1

--- a/solution.py
+++ b/solution.py
@@ -17,10 +17,9 @@
 BOX = 16.0
 HALF = 8.0
 KEYS = 48
-GROUP = 2
+GROUP = 8
 KERNEL_NORM = 21.0 / (2.0 * math.pi)
 GAMMA_LESS = 2.0 / 3.0
-STARTS = (0, 1024, 1280, 2048)
 
 NT = (((1,), (1,)), ((), ()))
 NN = (((1,), (0,)), ((), ()))
@@ -41,7 +40,18 @@
     return one, two, rest - two
 
 
-def dispatch_kernel(pos, mass, smooth, energy, dest, out):
+def first_kernel(count, *refs):
+    arguments, out, codes, held, done = refs[:6], refs[6], refs[7], refs[8:14], refs[14]
+    copies = [pltpu.make_async_copy(a, b, done.at[k]) for k, (a, b) in enumerate(zip(arguments, held))]
+    for copy in copies:
+        copy.start()
+    for copy in copies:
+        copy.wait()
+    dispatch(*held[:5], out)
+    list_pairs(count, held[5], codes)
+
+
+def dispatch(pos, mass, smooth, energy, dest, out):
     width = 256
     n = pos.shape[1]
     row = iota((width, width), 0)
@@ -68,11 +78,11 @@
     out[...] = total
 
 
-def list_kernel(count, pairs, out):
+def list_pairs(count, pairs, out):
     slots = pairs.shape[1]
     target, source = pairs[0:1, :], pairs[1:2, :]
     ghost = (source >= OWN).astype(I32)
-    line = jnp.where(iota((1, slots), 1) < count[0], target + OWN * ghost, -1)
+    line = jnp.where(iota((1, slots), 1) < count[0], 2 * target + ghost, -1)
     column = source - OWN * ghost
     lines = jnp.where(iota((ALL, slots), 0) == line, 1.0, 0.0).astype(BF16)
     columns = jnp.where(iota((OWN, slots), 0) == column, 1.0, 0.0).astype(BF16)
@@ -84,18 +94,14 @@
     per_line = dot(jnp.ones((OWN, OWN), BF16), has16)
     la, lb = iota((ALL, ALL), 0), iota((ALL, ALL), 1)
 
-    def section(k):
-        return (k >= OWN).astype(I32) + (k >= OWN + GT).astype(I32)
-
-    ahead = jnp.where((la < lb) & (section(la) == section(lb)), 1.0, 0.0).astype(BF16)
+    ahead = jnp.where(la < lb, 1.0, 0.0).astype(BF16)
     lane = iota((OWN, ALL), 1)
-    start = jnp.where(lane < OWN, STARTS[0], jnp.where(lane < OWN + GT, STARTS[1], STARTS[2]))
-    place = within + dot(per_line.astype(BF16), ahead) + start.astype(F32)
+    place = within + dot(per_line.astype(BF16), ahead)
     high = jnp.floor(place * (1.0 / 128.0))
     low = (place - 128.0 * high).astype(I32)
     high = jnp.where(has > 0.0, high.astype(I32), -1)
     sub = iota((OWN, ALL), 0)
-    code = times * 2048.0 + ((lane % OWN) * 64 + sub + jnp.where(lane >= OWN, OWN, 0)).astype(F32)
+    code = times * 2048.0 + ((lane // 2) * 64 + sub + (lane % 2) * OWN).astype(F32)
     total = jnp.zeros((48, 128), F32)
     parts = pieces(code)
     for k in range(OWN):
@@ -104,13 +110,8 @@
         right = jnp.where(iota((128, ALL), 0) == low[k : k + 1], 1.0, 0.0)
         total = total + dot(left.astype(BF16), right.astype(BF16), NT)
     out[0:16] = (total[0:16] + total[16:32] + total[32:48]).astype(I32)
-    lane1 = iota((1, ALL), 1)
-    tallies = []
-    for k in range(3):
-        tallies.append(jnp.sum(jnp.where(section(lane1) == k, per_line[0:1], 0.0), axis=1, keepdims=True))
-    r = iota((8, 128), 0)
-    counts = jnp.where(r == 0, tallies[0], jnp.where(r == 1, tallies[1], tallies[2]))
-    out[16:24] = counts.astype(I32)
+    tally = jnp.sum(per_line[0:1], axis=1, keepdims=True)
+    out[16:24] = jnp.broadcast_to(tally, (8, 128)).astype(I32)
 
 
 def fields_of(block, shift):
@@ -145,21 +146,20 @@
     return (code >> 6) & (OWN - 1), code & (ALL - 1), code >> 11
 
 
-def sweep(codes, section, product, process, buffers):
-    start = STARTS[section]
-    last = STARTS[section + 1] - 1
-    count = codes[16 + section, 0]
+def sweep(codes, product, process, buffers):
+    last = OWN * ALL - 1
+    count = codes[16, 0]
 
     def load(group, buffer):
         for k in range(GROUP):
-            t, s, _ = entry(codes, jnp.minimum(start + group * GROUP + k, last))
+            t, s, _ = entry(codes, jnp.minimum(group * GROUP + k, last))
             buffer[k] = product(t, s)
 
     def work(group, buffer):
         for k in range(GROUP):
-            e = start + group * GROUP + k
+            e = group * GROUP + k
             t, s, times = entry(codes, jnp.minimum(e, last))
-            process(t, s, jnp.where(e < start + count, times, 0), buffer, k)
+            process(t, s, jnp.where(e < count, times, 0), buffer, k)
 
     load(0, buffers[0])
 
@@ -195,14 +195,16 @@
         sums[tile] = none
         return unused
 
-    lax.fori_loop(0, OWN, own, 0)
+    lax.fori_loop(0, OWN, own, 0, unroll=8)
     for k, ghost in enumerate((g0, g1, g2, g3)):
+        there = jnp.full((8, 128), centre[2 + k], F32) > 0.0
 
         def other(tile, unused):
-            place(OWN + k * GT + tile, ghost[pl.ds(pl.multiple_of(tile * 8, 8), 8)])
+            block = ghost[pl.ds(pl.multiple_of(tile * 8, 8), 8)]
+            place(OWN + k * GT + tile, jnp.where(there, block, 0.0))
             return unused
 
-        lax.fori_loop(0, GT, other, 0)
+        lax.fori_loop(0, GT, other, 0, unroll=8)
 
     def product(t, s):
         return dot(factors[s], right[t])
@@ -216,8 +218,7 @@
         term = falloff * (ratio + 0.25) * buffer[k, :, 128:256]
         sums[t] += jnp.sum(term.reshape(16, 8, 128), axis=0) * jnp.full((8, 128), times, I32).astype(F32)
 
-    for section in range(3):
-        sweep(codes, section, product, process, (buf0, buf1))
+    sweep(codes, product, process, (buf0, buf1))
     total = jnp.sum(sums[...], axis=1)
     h = fields[0:OWN, 4, :]
     result = KERNEL_NORM / (h * h * h) * (total + fields[0:OWN, 3, :])
@@ -247,14 +248,14 @@
         sums[tile] = jnp.zeros((32, 128), F32)
         return unused
 
-    lax.fori_loop(0, OWN, own, 0)
+    lax.fori_loop(0, OWN, own, 0, unroll=8)
     for k, ghost in enumerate((p0, p1, p2, p3)):
 
         def other(tile, unused):
             pull(OWN + k * GT + tile, ghost[pl.ds(tile, 1)])
             return unused
 
-        lax.fori_loop(0, GT, other, 0)
+        lax.fori_loop(0, GT, other, 0, unroll=8)
 
     def product(t, s):
         return dot(factors[s], right[t])
@@ -270,8 +271,7 @@
         both = jnp.concatenate([first, second], axis=0)
         sums[t] += dot(pulls[s], both) * jnp.full((32, 128), times, I32).astype(F32)
 
-    for section in range(3):
-        sweep(codes, section, product, process, (buf0, buf1))
+    sweep(codes, product, process, (buf0, buf1))
 
     def finish(tile, unused):
         v = fields[tile]
@@ -285,9 +285,9 @@
     lax.fori_loop(0, OWN, finish, 0)
 
 
-def call(kernel, shapes, scratch=(), smem=0, args=(), limit=40):
+def call(kernel, shapes, scratch=(), smem=0, args=(), space=pltpu.VMEM, limit=40):
     specs = [pl.BlockSpec(memory_space=pltpu.SMEM)] * smem
-    specs += [pl.BlockSpec(memory_space=pltpu.VMEM)] * (len(args) - smem)
+    specs += [pl.BlockSpec(memory_space=space)] * (len(args) - smem)
     return pl.pallas_call(
         kernel,
         out_shape=[jax.ShapeDtypeStruct(s, d) for s, d in shapes],
@@ -302,7 +302,7 @@
     taken = []
     for axis in ("gx", "gy"):
         count = lax.axis_size(axis)
-        forward = [(i, i + 1) for i in range(count - 1)]
+        forward = [(i, (i + 1) % count) for i in range(count)]
         taken.append(lax.ppermute(edge, axis, forward))
         taken.append(lax.ppermute(edge, axis, [(b, a) for a, b in forward]))
     return taken
@@ -311,11 +311,21 @@
 def local(positions, mass, smoothing, energy, destination, pairs, pair_count):
     rows = mass.shape[0]
     flat = [a.reshape(1, rows) for a in (mass, smoothing, energy, destination)]
-    (outgoing,) = call(dispatch_kernel, [((256, 128), F32)], args=(positions, *flat))
-    (codes,) = call(list_kernel, [((24, 128), I32)], smem=1, args=(pair_count, pairs))
+    given = (positions, *flat, pairs)
+    outgoing, codes = call(
+        first_kernel,
+        [((256, 128), F32), ((24, 128), I32)],
+        scratch=[pltpu.VMEM(a.shape, a.dtype) for a in given] + [pltpu.SemaphoreType.DMA((len(given),))],
+        smem=1,
+        args=(pair_count, *given),
+        space=pl.ANY,
+        limit=60,
+    )
     moved = lax.all_to_all(outgoing, ("gx", "gy"), split_axis=0, concat_axis=0, tiled=True)
     ghosts = around(moved[: GT * 8])
-    centre = jnp.stack([lax.axis_index("gx"), lax.axis_index("gy")]).astype(F32) * BOX + HALF
+    i, j = lax.axis_index("gx"), lax.axis_index("gy")
+    there = [i > 0, i < lax.axis_size("gx") - 1, j > 0, j < lax.axis_size("gy") - 1]
+    centre = jnp.stack([i.astype(F32) * BOX + HALF, j.astype(F32) * BOX + HALF] + [t.astype(F32) for t in there])
     density, press, fields, factors = call(
         density_kernel,
         [((OWN, 128), F32), ((OWN, 128), F32), ((ALL, 8, 128), F32), ((ALL, 128, KEYS), BF16)],

time: 195 us -> 124 us (0.64)
  the two profiles are of different devices: /device:TPU:43 before, /device:TPU:1 now
where the time goes in v2:
time: 124 us; the launch traced here: 125 us
  Pallas kernels  77.8 us (63%)
  blocking collectives  28.7 us (23%)
  waiting for transfers between devices  10.1 us (8%)
  starting transfers between devices  6.42 us (5%)
  between operations  1.3 us (1%)
    pallas_call x3, Pallas kernels, call(): pl.pallas_call(kernel, out_shape=[jax.ShapeDtypeStruct(s, d) for s, d in...  77.8 us
    all_to_all x1, blocking collectives, local(): lax.all_to_all(outgoing, ('gx', 'gy'), split_axis=0, concat_axis=0, tiled...  28.7 us
    ppermute x4, waiting for transfers between devices, around(): taken.append(lax.ppermute(edge, axis, forward))  7.33 us
    ppermute x4, starting transfers between devices, around(): taken.append(lax.ppermute(edge, axis, forward))  5.13 us
    ppermute x4, waiting for transfers between devices, around(): taken.append(lax.ppermute(edge, axis, [(b, a) for a, b in forward]))  2.78 us
  transfers between devices with their start and end apart: 8, of which 4 were waited for; matrix products, arithmetic and copies ran while one was open for 0% of the time, Pallas kernels for 0%

profile of v2, /device:TPU:1, one launch (start us, length us, event | category | flops | bytes accessed | tf_op | source)
XLA Modules:
  0.0 125.0 jit_solution(16261711385707997314)
XLA Ops:
  1.3 5.9 %shard_map.86 = (f32[256,128]{1,0:T(8,128)}, s32[24,128]{1,0:T(8,128)}) custom-call(s32[1]{0:T(128)S(6)} %copy.11.count, f32[3,4096]{1,0:T(4,128)} %refs_0_.1, f32[1,4096]{1,0:T(1,128)} %bitcast.21, f32[1,4096]{1,0:T(1,128)} %bitcast.22, f32[1,4096]{1,0:T(1,128)} %bitcast.23, s32[1,4096]{1,0:T(1,128)} %bitcast.24, s32[2,864]{1,0:T(2,128)} %refs_5_.1), custom_call_target="tpu_custom_call" | custom-call | tf_op jit(solution)/shard_map/pallas_call | solution.py:291
  7.2 28.7 %all_to_all.11 = f32[256,1,128]{2,1,0:T(1,128)S(1)} all-to-all(f32[256,1,128]{2,1,0:T(1,128)} %bitcast.20), channel_id=1, replica_groups=mesh['gx'=32,'gy'=8] {'gx','gy'}, dimensions={0} | all-to-all | bytes 262144 | tf_op jit(solution)/shard_map/all_to_all | solution.py:324
  35.8 0.5 collective-permute-start.3
  36.3 1.3 %collective-permute-start.2 = (f32[64,128]{1,0:T(8,128)S(1)}, f32[64,128]{1,0:T(8,128)S(1)}, u32[]{:S(2)}, u32[]{:S(2)}) collective-permute-start(f32[64,128]{1,0:T(8,128)S(1)} %slice_bitcast_fusion), channel_id=1, source_target_pairs={{0,1},{1,2},{2,3},{3,4},{4,5},{5,6},{6,7},{7,0},{8,9},{9,10},{10,1... | collective-permute-start | bytes 98312 | tf_op jit(solution)/shard_map/ppermute | solution.py:306
  37.6 0.8 collective-permute-start.1
  38.4 0.7 collective-permute-start
  39.1 0.1 stack.43.centre
  39.1 0.0 collective-permute-done.3.g3
  39.2 0.0 collective-permute-done.2.g2
  39.2 1.7 %collective-permute-done.1.g1 = f32[64,128]{1,0:T(8,128)S(1)} collective-permute-done((f32[64,128]{1,0:T(8,128)S(1)}, f32[64,128]{1,0:T(8,128)S(1)}, u32[]{:S(2)}, u32[]{:S(2)}) %collective-permute-start.1) | collective-permute-done | bytes 32800 | tf_op jit(solution)/shard_map/ppermute | solution.py:307
  40.9 4.0 %collective-permute-done.g0 = f32[64,128]{1,0:T(8,128)S(1)} collective-permute-done((f32[64,128]{1,0:T(8,128)S(1)}, f32[64,128]{1,0:T(8,128)S(1)}, u32[]{:S(2)}, u32[]{:S(2)}) %collective-permute-start) | collective-permute-done | bytes 32800 | tf_op jit(solution)/shard_map/ppermute | solution.py:306
  44.9 0.0 copy-start
  44.9 0.7 copy-done
  45.6 32.9 %shard_map.87 = (f32[32,128]{1,0:T(8,128)}, f32[32,128]{1,0:T(8,128)S(1)}, f32[64,8,128]{2,1,0:T(8,128)S(1)}, bf16[64,128,48]{2,1,0:T(8,128)(2,1)S(1)}) custom-call(s32[24,128]{1,0:T(8,128)S(1)} %copy-done, f32[6]{0:T(128)S(1)} %stack.43.centre, f32[256,128]{1,0:T(8,128)S(1)} %bitcast.19, f32[64,128]{1,0:T(8,128)S(1)} %collective-permute-done.g0, ...), custom_call_target="tpu_custom_call" | custom-call | tf_op jit(solution)/shard_map/pallas_call | solution.py:291
  78.5 0.0 collective-permute-start.7
  78.5 1.7 %collective-permute-start.6 = (f32[8,128]{1,0:T(8,128)S(1)}, f32[8,128]{1,0:T(8,128)S(1)}, u32[]{:S(2)}, u32[]{:S(2)}) collective-permute-start(f32[8,128]{1,0:T(8,128)S(1)} %slice.11), channel_id=1, source_target_pairs={{0,1},{1,2},{2,3},{3,4},{4,5},{5,6},{6,7},{7,0},{8,9},{9,10},{10,1... | collective-permute-start | bytes 12296 | tf_op jit(solution)/shard_map/ppermute | solution.py:306
  80.3 0.0 collective-permute-start.5
  80.3 1.5 %collective-permute-start.4 = (f32[8,128]{1,0:T(8,128)S(1)}, f32[8,128]{1,0:T(8,128)S(1)}, u32[]{:S(2)}, u32[]{:S(2)}) collective-permute-start(f32[8,128]{1,0:T(8,128)S(1)} %slice.11), channel_id=1, source_target_pairs={{0,8},{8,16},{16,24},{24,32},{32,40},{40,48},{48,56},{56,64},{64,7... | collective-permute-start | bytes 12296 | tf_op jit(solution)/shard_map/ppermute | solution.py:306
  81.8 0.0 collective-permute-done.7.p3
  81.8 0.0 collective-permute-done.6.p2
  81.8 1.0 collective-permute-done.5.p1
  82.7 3.3 %collective-permute-done.4.p0 = f32[8,128]{1,0:T(8,128)S(1)} collective-permute-done((f32[8,128]{1,0:T(8,128)S(1)}, f32[8,128]{1,0:T(8,128)S(1)}, u32[]{:S(2)}, u32[]{:S(2)}) %collective-permute-start.4) | collective-permute-done | bytes 4128 | tf_op jit(solution)/shard_map/ppermute | solution.py:306
  86.1 39.0 %shard_map.88 = f32[3,4096]{1,0:T(4,128)} custom-call(s32[24,128]{1,0:T(8,128)S(1)} %copy-done, f32[64,8,128]{2,1,0:T(8,128)S(1)} %get-tuple-element.11.fields, bf16[64,128,48]{2,1,0:T(8,128)(2,1)S(1)} %get-tuple-element.12.factors, f32[32,128]{1,0:T(8,128)S(1)} %get-tuple-element.13.press, f32[8,128]{1,0:T(8,128)S(1)} %collective-permute-done.4.p0, ...), custom_call_target="tpu_custom_call" | custom-call | tf_op jit(solution)/shard_map/pallas_call | solution.py:291
  (2 shorter events, 0.0 us)
Async XLA Ops:
  35.8 3.3 %collective-permute-start.3 = (f32[64,128]{1,0:T(8,128)S(1)}, f32[64,128]{1,0:T(8,128)S(1)}, u32[]{:S(2)}, u32[]{:S(2)}) collective-permute-start(f32[64,128]{1,0:T(8,128)S(1)} %slice_bitcast_fusion), channel_id=1, source_target_pairs={{1,0},{2,1},{3,2},{4,3},{5,4},{6,5},{7,6},{0,7},{9,8},{10,9},{11,1... | collective-permute-start | bytes 98312 | tf_op jit(solution)/shard_map/ppermute | solution.py:307
  36.3 2.9 %collective-permute-start.2 = (f32[64,128]{1,0:T(8,128)S(1)}, f32[64,128]{1,0:T(8,128)S(1)}, u32[]{:S(2)}, u32[]{:S(2)}) collective-permute-start(f32[64,128]{1,0:T(8,128)S(1)} %slice_bitcast_fusion), channel_id=1, source_target_pairs={{0,1},{1,2},{2,3},{3,4},{4,5},{5,6},{6,7},{7,0},{8,9},{9,10},{10,1... | collective-permute-start | bytes 98312 | tf_op jit(solution)/shard_map/ppermute | solution.py:306
  37.6 3.3 %collective-permute-start.1 = (f32[64,128]{1,0:T(8,128)S(1)}, f32[64,128]{1,0:T(8,128)S(1)}, u32[]{:S(2)}, u32[]{:S(2)}) collective-permute-start(f32[64,128]{1,0:T(8,128)S(1)} %slice_bitcast_fusion), channel_id=1, source_target_pairs={{8,0},{16,8},{24,16},{32,24},{40,32},{48,40},{56,48},{64,56},{72,6... | collective-permute-start | bytes 98312 | tf_op jit(solution)/shard_map/ppermute | solution.py:307
  38.4 6.5 %collective-permute-start = (f32[64,128]{1,0:T(8,128)S(1)}, f32[64,128]{1,0:T(8,128)S(1)}, u32[]{:S(2)}, u32[]{:S(2)}) collective-permute-start(f32[64,128]{1,0:T(8,128)S(1)} %slice_bitcast_fusion), channel_id=1, source_target_pairs={{0,8},{8,16},{16,24},{24,32},{32,40},{40,48},{48,56},{56,64},{64,7... | collective-permute-start | bytes 98312 | tf_op jit(solution)/shard_map/ppermute | solution.py:306
  44.9 0.7 copy-start
  78.5 3.2 %collective-permute-start.7 = (f32[8,128]{1,0:T(8,128)S(1)}, f32[8,128]{1,0:T(8,128)S(1)}, u32[]{:S(2)}, u32[]{:S(2)}) collective-permute-start(f32[8,128]{1,0:T(8,128)S(1)} %slice.11), channel_id=1, source_target_pairs={{1,0},{2,1},{3,2},{4,3},{5,4},{6,5},{7,6},{0,7},{9,8},{10,9},{11,1... | collective-permute-start | bytes 12296 | tf_op jit(solution)/shard_map/ppermute | solution.py:307
  78.5 3.2 %collective-permute-start.6 = (f32[8,128]{1,0:T(8,128)S(1)}, f32[8,128]{1,0:T(8,128)S(1)}, u32[]{:S(2)}, u32[]{:S(2)}) collective-permute-start(f32[8,128]{1,0:T(8,128)S(1)} %slice.11), channel_id=1, source_target_pairs={{0,1},{1,2},{2,3},{3,4},{4,5},{5,6},{6,7},{7,0},{8,9},{9,10},{10,1... | collective-permute-start | bytes 12296 | tf_op jit(solution)/shard_map/ppermute | solution.py:306
  80.3 2.5 %collective-permute-start.5 = (f32[8,128]{1,0:T(8,128)S(1)}, f32[8,128]{1,0:T(8,128)S(1)}, u32[]{:S(2)}, u32[]{:S(2)}) collective-permute-start(f32[8,128]{1,0:T(8,128)S(1)} %slice.11), channel_id=1, source_target_pairs={{8,0},{16,8},{24,16},{32,24},{40,32},{48,40},{56,48},{64,56},{72,6... | collective-permute-start | bytes 12296 | tf_op jit(solution)/shard_map/ppermute | solution.py:307
  80.3 5.8 %collective-permute-start.4 = (f32[8,128]{1,0:T(8,128)S(1)}, f32[8,128]{1,0:T(8,128)S(1)}, u32[]{:S(2)}, u32[]{:S(2)}) collective-permute-start(f32[8,128]{1,0:T(8,128)S(1)} %slice.11), channel_id=1, source_target_pairs={{0,8},{8,16},{16,24},{24,32},{32,40},{40,48},{48,56},{56,64},{64,7... | collective-permute-start | bytes 12296 | tf_op jit(solution)/shard_map/ppermute | solution.py:306

commit v3 on v2

--- a/solution.py
+++ b/solution.py
@@ -17,7 +17,7 @@
 BOX = 16.0
 HALF = 8.0
 KEYS = 48
-GROUP = 8
+DEPTH = (24, 20)
 KERNEL_NORM = 21.0 / (2.0 * math.pi)
 GAMMA_LESS = 2.0 / 3.0
 
@@ -147,33 +147,37 @@
 
 
 def sweep(codes, product, process, buffers):
+    turns, depth = len(buffers), buffers[0].shape[0]
     last = OWN * ALL - 1
     count = codes[16, 0]
 
-    def load(group, buffer):
-        for k in range(GROUP):
-            t, s, _ = entry(codes, jnp.minimum(group * GROUP + k, last))
-            buffer[k] = product(t, s)
-
-    def work(group, buffer):
-        for k in range(GROUP):
-            e = group * GROUP + k
-            t, s, times = entry(codes, jnp.minimum(e, last))
-            process(t, s, jnp.where(e < count, times, 0), buffer, k)
-
-    load(0, buffers[0])
+    def load(e, buffer, k):
+        t, s, _ = entry(codes, jnp.minimum(e, last))
+        buffer[k] = product(t, s)
+
+    def work(e, buffer, k):
+        t, s, times = entry(codes, jnp.minimum(e, last))
+        process(t, s, jnp.where(e < count, times, 0), buffer, k)
+
+    for k in range(depth):
+        load(k, buffers[0], k)
 
     def body(i, unused):
-        load(2 * i + 1, buffers[1])
-        work(2 * i, buffers[0])
-        load(2 * i + 2, buffers[0])
-        work(2 * i + 1, buffers[1])
+        for turn in range(turns):
+            for k in range(depth):
+                e = (i * turns + turn) * depth + k
+                if turns == 1:
+                    work(e, buffers[0], k)
+                    load(e + depth, buffers[0], k)
+                else:
+                    load(e + depth, buffers[1 - turn], k)
+                    work(e, buffers[turn], k)
         return unused
 
-    lax.fori_loop(0, (count + 2 * GROUP - 1) // (2 * GROUP), body, 0)
-
-
-def density_kernel(codes, centre, moved, g0, g1, g2, g3, density, press, fields, factors, right, sums, buf0, buf1):
+    lax.fori_loop(0, (count + turns * depth - 1) // (turns * depth), body, 0)
+
+
+def density_kernel(codes, centre, moved, g0, g1, g2, g3, density, press, fields, factors, right, sums, buffer):
     sub = iota((8, 128), 0)
     shift = jnp.where(sub == 0, centre[0], jnp.where(sub == 1, centre[1], jnp.where(sub == 2, HALF, 0.0)))
 
@@ -218,7 +222,7 @@
         term = falloff * (ratio + 0.25) * buffer[k, :, 128:256]
         sums[t] += jnp.sum(term.reshape(16, 8, 128), axis=0) * jnp.full((8, 128), times, I32).astype(F32)
 
-    sweep(codes, product, process, (buf0, buf1))
+    sweep(codes, product, process, (buffer,))
     total = jnp.sum(sums[...], axis=1)
     h = fields[0:OWN, 4, :]
     result = KERNEL_NORM / (h * h * h) * (total + fields[0:OWN, 3, :])
@@ -242,7 +246,7 @@
 
     def own(tile, unused):
         v = pull(tile, press[pl.ds(tile, 1)])
-        right[tile, :, 0:128] = target_factor(coefficients(v)).astype(BF16)
+        right[tile, :, 0:128] = target_factor(4.0 * coefficients(v)).astype(BF16)
         h = jnp.where(sub == 4, 1.0, jnp.where(sub == 7, v[4:5], 0.0))
         right[tile, :, 128:256] = target_factor(h).astype(BF16)
         sums[tile] = jnp.zeros((32, 128), F32)
@@ -264,7 +268,7 @@
         dist_sq = jnp.maximum(buffer[k, :, 0:128], 1e-30)
         near = 1.0 / buffer[k, :, 128:256]
         near_sq = near * near
-        gap = jnp.maximum(near - dist_sq * lax.rsqrt(dist_sq) * (2.0 * near_sq), 0.0)
+        gap = jnp.maximum(near - dist_sq * lax.rsqrt(dist_sq) * near_sq, 0.0)
         slope = gap * gap * gap * near_sq
         first = slope.astype(BF16)
         second = (slope - first.astype(F32)).astype(BF16)
@@ -332,8 +336,7 @@
         scratch=[
             pltpu.VMEM((OWN, KEYS, 256), BF16),
             pltpu.VMEM((OWN, 8, 128), F32),
-            pltpu.VMEM((GROUP, 128, 256), F32),
-            pltpu.VMEM((GROUP, 128, 256), F32),
+            pltpu.VMEM((DEPTH[0], 128, 256), F32),
         ],
         smem=2,
         args=(codes, centre, moved, *ghosts),
@@ -346,8 +349,8 @@
             pltpu.VMEM((OWN, KEYS, 256), BF16),
             pltpu.VMEM((ALL, 32, 256), BF16),
             pltpu.VMEM((OWN, 32, 128), F32),
-            pltpu.VMEM((GROUP, 128, 256), F32),
-            pltpu.VMEM((GROUP, 128, 256), F32),
+            pltpu.VMEM((DEPTH[1], 128, 256), F32),
+            pltpu.VMEM((DEPTH[1], 128, 256), F32),
         ],
         smem=1,
         args=(codes, fields, factors, press, *presses),

time: 124 us -> 108 us (0.87)
  the two profiles are of different devices: /device:TPU:1 before, /device:TPU:2 now
where the time goes in v3:
time: 108 us; the launch traced here: 109 us
  Pallas kernels  62.8 us (58%)
  blocking collectives  26.7 us (25%)
  waiting for transfers between devices  11.6 us (11%)
  starting transfers between devices  5.66 us (5%)
  between operations  1.3 us (1%)
    pallas_call x3, Pallas kernels, call(): pl.pallas_call(kernel, out_shape=[jax.ShapeDtypeStruct(s, d) for s, d in...  62.8 us
    all_to_all x1, blocking collectives, local(): lax.all_to_all(outgoing, ('gx', 'gy'), split_axis=0, concat_axis=0, tiled...  26.7 us
    ppermute x4, waiting for transfers between devices, around(): taken.append(lax.ppermute(edge, axis, forward))  9.94 us
    ppermute x4, starting transfers between devices, around(): taken.append(lax.ppermute(edge, axis, forward))  2.97 us
    ppermute x4, starting transfers between devices, around(): taken.append(lax.ppermute(edge, axis, [(b, a) for a, b in forward]))  2.69 us
  transfers between devices with their start and end apart: 8, of which 6 were waited for; matrix products, arithmetic and copies ran while one was open for 0% of the time, Pallas kernels for 0%

profile of v3, /device:TPU:2, one launch (start us, length us, event | category | flops | bytes accessed | tf_op | source)
XLA Modules:
  0.0 108.9 jit_solution(16386643745992910751)
XLA Ops:
  1.3 5.9 %shard_map.86 = (f32[256,128]{1,0:T(8,128)}, s32[24,128]{1,0:T(8,128)}) custom-call(s32[1]{0:T(128)S(6)} %copy.11.count, f32[3,4096]{1,0:T(4,128)} %refs_0_.1, f32[1,4096]{1,0:T(1,128)} %bitcast.21, f32[1,4096]{1,0:T(1,128)} %bitcast.22, f32[1,4096]{1,0:T(1,128)} %bitcast.23, s32[1,4096]{1,0:T(1,128)} %bitcast.24, s32[2,864]{1,0:T(2,128)} %refs_5_.1), custom_call_target="tpu_custom_call" | custom-call | tf_op jit(solution)/shard_map/pallas_call | solution.py:295
  7.2 26.7 %all_to_all.11 = f32[256,1,128]{2,1,0:T(1,128)S(1)} all-to-all(f32[256,1,128]{2,1,0:T(1,128)} %bitcast.20), channel_id=1, replica_groups=mesh['gx'=32,'gy'=8] {'gx','gy'}, dimensions={0} | all-to-all | bytes 262144 | tf_op jit(solution)/shard_map/all_to_all | solution.py:328
  33.9 1.1 collective-permute-start.3
  35.0 0.0 collective-permute-start.2
  35.0 1.1 collective-permute-start.1
  36.1 1.0 collective-permute-start
  37.0 0.1 stack.43.centre
  37.1 0.0 collective-permute-done.3.g3
  37.1 1.2 %collective-permute-done.2.g2 = f32[64,128]{1,0:T(8,128)S(1)} collective-permute-done((f32[64,128]{1,0:T(8,128)S(1)}, f32[64,128]{1,0:T(8,128)S(1)}, u32[]{:S(2)}, u32[]{:S(2)}) %collective-permute-start.2) | collective-permute-done | bytes 32800 | tf_op jit(solution)/shard_map/ppermute | solution.py:310
  38.3 0.6 collective-permute-done.1.g1
  38.9 4.4 %collective-permute-done.g0 = f32[64,128]{1,0:T(8,128)S(1)} collective-permute-done((f32[64,128]{1,0:T(8,128)S(1)}, f32[64,128]{1,0:T(8,128)S(1)}, u32[]{:S(2)}, u32[]{:S(2)}) %collective-permute-start) | collective-permute-done | bytes 32800 | tf_op jit(solution)/shard_map/ppermute | solution.py:310
  43.3 0.0 copy-start
  43.3 0.7 copy-done
  44.0 27.9 %shard_map.87 = (f32[32,128]{1,0:T(8,128)}, f32[32,128]{1,0:T(8,128)S(1)}, f32[64,8,128]{2,1,0:T(8,128)S(1)}, bf16[64,128,48]{2,1,0:T(8,128)(2,1)S(1)}) custom-call(s32[24,128]{1,0:T(8,128)S(1)} %copy-done, f32[6]{0:T(128)S(1)} %stack.43.centre, f32[256,128]{1,0:T(8,128)S(1)} %bitcast.19, f32[64,128]{1,0:T(8,128)S(1)} %collective-permute-done.g0, ...), custom_call_target="tpu_custom_call" | custom-call | tf_op jit(solution)/shard_map/pallas_call | solution.py:295
  71.9 0.0 collective-permute-start.7
  71.9 0.5 collective-permute-start.6
  72.4 0.5 collective-permute-start.5
  72.9 1.5 %collective-permute-start.4 = (f32[8,128]{1,0:T(8,128)S(1)}, f32[8,128]{1,0:T(8,128)S(1)}, u32[]{:S(2)}, u32[]{:S(2)}) collective-permute-start(f32[8,128]{1,0:T(8,128)S(1)} %slice.11), channel_id=1, source_target_pairs={{0,8},{8,16},{16,24},{24,32},{32,40},{40,48},{48,56},{56,64},{64,7... | collective-permute-start | bytes 12296 | tf_op jit(solution)/shard_map/ppermute | solution.py:310
  74.4 0.0 collective-permute-done.7.p3
  74.4 0.5 collective-permute-done.6.p2
  74.9 1.1 collective-permute-done.5.p1
  76.0 3.8 %collective-permute-done.4.p0 = f32[8,128]{1,0:T(8,128)S(1)} collective-permute-done((f32[8,128]{1,0:T(8,128)S(1)}, f32[8,128]{1,0:T(8,128)S(1)}, u32[]{:S(2)}, u32[]{:S(2)}) %collective-permute-start.4) | collective-permute-done | bytes 4128 | tf_op jit(solution)/shard_map/ppermute | solution.py:310
  79.9 29.0 %shard_map.88 = f32[3,4096]{1,0:T(4,128)} custom-call(s32[24,128]{1,0:T(8,128)S(1)} %copy-done, f32[64,8,128]{2,1,0:T(8,128)S(1)} %get-tuple-element.11.fields, bf16[64,128,48]{2,1,0:T(8,128)(2,1)S(1)} %get-tuple-element.12.factors, f32[32,128]{1,0:T(8,128)S(1)} %get-tuple-element.13.press, f32[8,128]{1,0:T(8,128)S(1)} %collective-permute-done.4.p0, ...), custom_call_target="tpu_custom_call" | custom-call | tf_op jit(solution)/shard_map/pallas_call | solution.py:295
  (2 shorter events, 0.0 us)
Async XLA Ops:
  33.9 3.2 %collective-permute-start.3 = (f32[64,128]{1,0:T(8,128)S(1)}, f32[64,128]{1,0:T(8,128)S(1)}, u32[]{:S(2)}, u32[]{:S(2)}) collective-permute-start(f32[64,128]{1,0:T(8,128)S(1)} %slice_bitcast_fusion), channel_id=1, source_target_pairs={{1,0},{2,1},{3,2},{4,3},{5,4},{6,5},{7,6},{0,7},{9,8},{10,9},{11,1... | collective-permute-start | bytes 98312 | tf_op jit(solution)/shard_map/ppermute | solution.py:311
  35.0 3.3 %collective-permute-start.2 = (f32[64,128]{1,0:T(8,128)S(1)}, f32[64,128]{1,0:T(8,128)S(1)}, u32[]{:S(2)}, u32[]{:S(2)}) collective-permute-start(f32[64,128]{1,0:T(8,128)S(1)} %slice_bitcast_fusion), channel_id=1, source_target_pairs={{0,1},{1,2},{2,3},{3,4},{4,5},{5,6},{6,7},{7,0},{8,9},{9,10},{10,1... | collective-permute-start | bytes 98312 | tf_op jit(solution)/shard_map/ppermute | solution.py:310
  35.0 4.0 %collective-permute-start.1 = (f32[64,128]{1,0:T(8,128)S(1)}, f32[64,128]{1,0:T(8,128)S(1)}, u32[]{:S(2)}, u32[]{:S(2)}) collective-permute-start(f32[64,128]{1,0:T(8,128)S(1)} %slice_bitcast_fusion), channel_id=1, source_target_pairs={{8,0},{16,8},{24,16},{32,24},{40,32},{48,40},{56,48},{64,56},{72,6... | collective-permute-start | bytes 98312 | tf_op jit(solution)/shard_map/ppermute | solution.py:311
  36.1 7.3 %collective-permute-start = (f32[64,128]{1,0:T(8,128)S(1)}, f32[64,128]{1,0:T(8,128)S(1)}, u32[]{:S(2)}, u32[]{:S(2)}) collective-permute-start(f32[64,128]{1,0:T(8,128)S(1)} %slice_bitcast_fusion), channel_id=1, source_target_pairs={{0,8},{8,16},{16,24},{24,32},{32,40},{40,48},{48,56},{56,64},{64,7... | collective-permute-start | bytes 98312 | tf_op jit(solution)/shard_map/ppermute | solution.py:310
  43.3 0.7 copy-start
  71.9 2.5 %collective-permute-start.7 = (f32[8,128]{1,0:T(8,128)S(1)}, f32[8,128]{1,0:T(8,128)S(1)}, u32[]{:S(2)}, u32[]{:S(2)}) collective-permute-start(f32[8,128]{1,0:T(8,128)S(1)} %slice.11), channel_id=1, source_target_pairs={{1,0},{2,1},{3,2},{4,3},{5,4},{6,5},{7,6},{0,7},{9,8},{10,9},{11,1... | collective-permute-start | bytes 12296 | tf_op jit(solution)/shard_map/ppermute | solution.py:311
  71.9 3.0 %collective-permute-start.6 = (f32[8,128]{1,0:T(8,128)S(1)}, f32[8,128]{1,0:T(8,128)S(1)}, u32[]{:S(2)}, u32[]{:S(2)}) collective-permute-start(f32[8,128]{1,0:T(8,128)S(1)} %slice.11), channel_id=1, source_target_pairs={{0,1},{1,2},{2,3},{3,4},{4,5},{5,6},{6,7},{7,0},{8,9},{9,10},{10,1... | collective-permute-start | bytes 12296 | tf_op jit(solution)/shard_map/ppermute | solution.py:310
  72.4 3.6 %collective-permute-start.5 = (f32[8,128]{1,0:T(8,128)S(1)}, f32[8,128]{1,0:T(8,128)S(1)}, u32[]{:S(2)}, u32[]{:S(2)}) collective-permute-start(f32[8,128]{1,0:T(8,128)S(1)} %slice.11), channel_id=1, source_target_pairs={{8,0},{16,8},{24,16},{32,24},{40,32},{48,40},{56,48},{64,56},{72,6... | collective-permute-start | bytes 12296 | tf_op jit(solution)/shard_map/ppermute | solution.py:311
  72.9 6.9 %collective-permute-start.4 = (f32[8,128]{1,0:T(8,128)S(1)}, f32[8,128]{1,0:T(8,128)S(1)}, u32[]{:S(2)}, u32[]{:S(2)}) collective-permute-start(f32[8,128]{1,0:T(8,128)S(1)} %slice.11), channel_id=1, source_target_pairs={{0,8},{8,16},{16,24},{24,32},{32,40},{40,48},{48,56},{56,64},{64,7... | collective-permute-start | bytes 12296 | tf_op jit(solution)/shard_map/ppermute | solution.py:310
